TPU v7x, 256 devices: a whole 4x4x8 slice. The times are simulated.
256 devices in a mesh: section: 8 (over x, y_lo), dp: 32 (over z, y_hi, core).
Axes of the slice: x: 4, y: 4 (y_hi: 2, y_lo: 2; y = y_hi * 2 + y_lo), z: 8, core: 2. Of those that a mesh axis runs over, the one named last changes fastest.
Arguments:
- act_sent: bfloat16 [8, 4096, 6144], P('section', 'dp'), may hold values from -6 to 6
- grad_sent: bfloat16 [8, 4096, 6144], P('section', 'dp'), may hold values from -6 to 6
- stash_pool: bfloat16 [8, 2, 4096, 6144], P('section', None, 'dp'), may hold values from -6 to 6
- w_in: bfloat16 [8, 6144, 384], P('section', 'dp'), may hold values from -0.078125 to 0.078125
- w_out: bfloat16 [8, 384, 6144], P('section', None, 'dp'), may hold values from -0.3125 to 0.3125
- gain: bfloat16 [8, 6144], P('section', 'dp'), may hold values from 0.5 to 1.5
- plan: int32 [8, 2], replicated, may hold values from 0 to 3, as said below
Outputs:
- act_next: bfloat16 [8, 4096, 6144], P('section', 'dp')
- grad_next: bfloat16 [8, 4096, 6144], P('section', 'dp')
- pool_next: bfloat16 [8, 2, 4096, 6144], P('section', None, 'dp')
- grad_w_in: float32 [8, 6144, 384], P('section', 'dp')
- grad_w_out: float32 [8, 384, 6144], P('section', None, 'dp')
- grad_gain: float32 [8, 6144], P('section', 'dp')
Inputs may be any that keep to these rules, and one draw needn't show every extreme that they name: `plan`: for sections s < 4 the first column is 2 or 3 and the second is 2 or 3. For each pair s, m = 7 - s, the two sections' second columns name different slots of the pair's four.
All inputs are finite; a program needn't handle non-finite values.
Results may differ from a plain program's by a relative error of at most 0.023.
Values may be sent and summed in bfloat16 or wider, within the bound.
A program may use at most 128 MiB of HBM per device.

v0:
```python
import jax
import jax.numpy as jnp
from jax import lax
from jax.sharding import PartitionSpec as P

EPSILON = 1e-05
CONTRACT_ROWS = (((0,), (0,)), ((), ()))
CONTRACT_COLS = (((1,), (1,)), ((), ()))


def from_behind(value, axis, steps):
    count = lax.axis_size(axis)
    pairs = [(source, (source + steps) % count) for source in range(count)]
    return lax.ppermute(value, axis, pairs)


def partner_2(block, axis, bit):
    count = lax.axis_size(axis)
    route = []
    for low in range(count):
        high = low | 1 << bit
        if high != low and high < count:
            route += [(low, high), (high, low)]
    return lax.ppermute(block, axis, route)


def unit_rows(rows):
    values = rows.astype(jnp.float32)
    average = jnp.mean(values, axis=-1, keepdims=True)
    centred = values - average
    inverse = lax.rsqrt(jnp.mean(centred * centred, axis=-1, keepdims=True) + EPSILON)
    return (centred * inverse, inverse)


def gelu_tangent(pre_act, upstream):
    _, pullback = jax.vjp(jax.nn.gelu, pre_act)
    return pullback(upstream)[0]


def per_device(act_sent, grad_sent, stash_pool, w_in, w_out, gain, plan):
    sections = lax.axis_size("section")
    position = lax.axis_index("section")
    partner = sections - 1 - position
    inputs = from_behind(act_sent, "section", 1)[0]
    upstream = from_behind(grad_sent, "section", -1)[0]
    gain_full, w_in_full, w_out_full = (
        lax.all_gather(gain, "dp", axis=1, tiled=True),
        lax.all_gather(w_in, "dp", axis=1, tiled=True),
        lax.all_gather(w_out, "dp", axis=2, tiled=True),
    )
    gain_row = gain_full[0].astype(jnp.float32)
    w_in_full = w_in_full[0]
    w_out_full = w_out_full[0]
    pool_here = stash_pool[0]
    my_codes = lax.dynamic_index_in_dim(plan, position, 0, keepdims=False)
    partner_codes = lax.dynamic_index_in_dim(plan, partner, 0, keepdims=False)
    wanted = lax.dynamic_index_in_dim(
        pool_here, jnp.maximum(partner_codes[0] - 2, 0), 0, keepdims=False
    )
    payload = jnp.stack([wanted, inputs])
    row_count = inputs.shape[0]
    bit_count = sections.bit_length() - 1
    for bit_index in range(bit_count):
        payload = partner_2(payload, "section", bit_index)
    far_slot = payload[0]
    partner_inputs = payload[1]
    own_slot = lax.dynamic_index_in_dim(pool_here, jnp.minimum(my_codes[0], 1), 0, keepdims=False)
    stashed = jnp.where(my_codes[0] >= 2, far_slot, own_slot)
    slot_list = [
        jnp.where(
            my_codes[1] == slot_index,
            inputs,
            jnp.where(partner_codes[1] == slot_index + 2, partner_inputs, pool_here[slot_index]),
        )
        for slot_index in range(pool_here.shape[0])
    ]
    pool_next = jnp.stack(slot_list)
    stacked = jnp.concatenate([inputs, stashed], axis=0)
    unit_all, inverse_all = unit_rows(stacked)
    normed_all = (unit_all * gain_row).astype(jnp.bfloat16)
    pre_all = jnp.dot(normed_all, w_in_full, preferred_element_type=jnp.float32)
    hidden_x = jax.nn.gelu(pre_all[:row_count]).astype(jnp.bfloat16)
    forward = (
        inputs.astype(jnp.float32)
        + jnp.dot(hidden_x, w_out_full, preferred_element_type=jnp.float32)
    ).astype(jnp.bfloat16)
    unit_z = unit_all[row_count:]
    inverse_z = inverse_all[row_count:]
    normed_z = normed_all[row_count:]
    pre_z = pre_all[row_count:]
    hidden_z = jax.nn.gelu(pre_z).astype(jnp.bfloat16)
    part_out = lax.dot_general(
        hidden_z, upstream, CONTRACT_ROWS, preferred_element_type=jnp.float32
    )
    d_hidden = lax.dot_general(
        upstream, w_out_full, CONTRACT_COLS, preferred_element_type=jnp.float32
    )
    d_pre = gelu_tangent(pre_z, d_hidden).astype(jnp.bfloat16)
    part_in = lax.dot_general(normed_z, d_pre, CONTRACT_ROWS, preferred_element_type=jnp.float32)
    d_normed = lax.dot_general(d_pre, w_in_full, CONTRACT_COLS, preferred_element_type=jnp.float32)
    part_gain = jnp.sum(d_normed * unit_z, axis=0)
    d_unit = d_normed * gain_row
    d_input = inverse_z * (
        d_unit
        - jnp.mean(d_unit, axis=-1, keepdims=True)
        - unit_z * jnp.mean(d_unit * unit_z, axis=-1, keepdims=True)
    )
    backward = (upstream.astype(jnp.float32) + d_input).astype(jnp.bfloat16)
    sum_in, sum_out, sum_gain = (
        lax.psum_scatter(
            part_in.astype(jnp.bfloat16), "dp", scatter_dimension=0, tiled=True
        ).astype(jnp.float32),
        lax.psum_scatter(
            part_out.astype(jnp.bfloat16), "dp", scatter_dimension=1, tiled=True
        ).astype(jnp.float32),
        lax.psum_scatter(
            part_gain.astype(jnp.bfloat16), "dp", scatter_dimension=0, tiled=True
        ).astype(jnp.float32),
    )
    return (
        forward[None],
        backward[None],
        pool_next[None],
        sum_in[None],
        sum_out[None],
        sum_gain[None],
    )


def solution(mesh):
    placed = (
        P("section", "dp", None),
        P("section", "dp", None),
        P("section", None, "dp", None),
        P("section", "dp", None),
        P("section", None, "dp"),
        P("section", "dp"),
        P(),
    )
    return jax.shard_map(
        per_device,
        mesh=mesh,
        in_specs=placed,
        out_specs=(
            P("section", "dp", None),
            P("section", "dp", None),
            P("section", None, "dp", None),
            P("section", "dp", None),
            P("section", None, "dp"),
            P("section", "dp"),
        ),
        check_vma=False,
    )
```

profile of v0, /device:TPU:224, one launch (start us, length us, event | category | flops | bytes accessed | tf_op | source)
XLA Modules:
  0.0 643.4 jit_solution(1833120545231083649)
XLA Ops:
  7.9 1.7 collective-permute-start
  11.6 1.5 dynamic-slice_bitcast_fusion
  13.2 33.4 %collective-permute-done = bf16[1,128,6144]{2,1,0:T(8,128)(2,1)S(1)} collective-permute-done((bf16[1,128,6144]{2,1,0:T(8,128)(2,1)}, bf16[1,128,6144]{2,1,0:T(8,128)(2,1)S(1)}, u32[]{:S(2)}, u32[]{:S(2)}) %collective-permute-start) | collective-permute-done | bytes 1572896 | tf_op jit(solution)/shard_map/ppermute | solution.py:14
  47.9 80.7 %collective-permute-done.1 = bf16[2,128,6144]{2,1,0:T(8,128)(2,1)} collective-permute-done((bf16[2,128,6144]{2,1,0:T(8,128)(2,1)S(1)}, bf16[2,128,6144]{2,1,0:T(8,128)(2,1)}, u32[]{:S(2)}, u32[]{:S(2)}) %collective-permute-start.1) | collective-permute-done | bytes 3145760 | tf_op jit(solution)/shard_map/ppermute | solution.py:24
  129.5 67.4 %collective-permute-done.2 = bf16[2,128,6144]{2,1,0:T(8,128)(2,1)} collective-permute-done((bf16[2,128,6144]{2,1,0:T(8,128)(2,1)}, bf16[2,128,6144]{2,1,0:T(8,128)(2,1)}, u32[]{:S(2)}, u32[]{:S(2)}) %collective-permute-start.2) | collective-permute-done | bytes 3145760 | tf_op jit(solution)/shard_map/ppermute | solution.py:24
  196.9 2.8 collective-permute-start.3
  199.8 2.0 collective-permute-start.4
  204.6 134.5 %all-reduce = bf16[6144]{0:T(1024)(128)(2,1)S(1)} all-reduce(bf16[6144]{0:T(1024)(128)(2,1)S(1)} %dynamic-update-slice), channel_id=1, replica_groups=mesh['section'=8,'dp'=32] {'dp'}, use_global_device_ids=true, to_apply=%add | all-reduce | flops 6144 | bytes 24576
  339.2 2.0 fusion.14
  342.7 4.9 fusion
  347.6 5.8 fusion.9
  353.5 3.5 fusion.25
  357.0 3.6 convolution_convert_fusion.1
  360.9 4.5 convolution_convert_fusion
  368.7 6.7 %multiply_reduce_fusion = (bf16[6144]{0:T(1024)(128)(2,1)S(1)}, f32[128]{0:T(128)S(1)}, f32[128]{0:T(128)S(1)}, f32[128,6144]{1,0:T(8,128)}) fusion(f32[256,6144]{1,0:T(8,128)} %get-tuple-element.11, f32[6144]{0:T(1024)S(1)} %mul.148, bf16[128,384]{1,0:T(8,128)(2,1)S(1)} %fusion.25, bf16[1,6144,384]{2,1,0:T(8,128)(2,1)} %all-gather.3.cloned.1.call-done), kind=kOutput, calls=%fused_computation.19 | convolution fusion | flops 608691968 | bytes 11146240 | tf_op jit(solution)/shard_map/dot_general | solution.py:100
  375.4 127.4 %all-reduce.1 = bf16[6144]{0:T(1024)(128)(2,1)S(1)} all-reduce(bf16[6144]{0:T(1024)(128)(2,1)S(1)} %get-tuple-element.6), channel_id=4, replica_groups=mesh['section'=8,'dp'=32] {'dp'}, use_global_device_ids=true, to_apply=%region_7.8.clone | all-reduce | flops 6144 | bytes 24576
  503.4 5.3 fusion.11
  508.8 1.9 fusion.16
  510.7 1.9 maximum_bitcast_fusion
  512.7 1.1 copy-done.1
  513.8 2.3 fusion.12
  516.0 1.7 bitcast_convert_fusion.1
  517.7 117.5 %reduce-scatter.5.cloned.1.call-done = bf16[384,192]{0,1:T(8,128)(2,1)} async-done(((bf16[384,6144]{0,1:T(8,128)(2,1)}), bf16[384,192]{0,1:T(8,128)(2,1)}) %reduce-scatter.5.cloned.1.call-update) | async-done | bytes 147472 | tf_op jit(solution)/shard_map/reduce_scatter | solution.py:113
  635.2 1.6 bitcast_convert_fusion
  (45 shorter events, 7.6 us)
Async XLA Ops:
  7.2 340.5 %all-gather.3.cloned.1.call-start = ((), (), s32[]{:S(2)}) async-start(), calls=%async_computation.2 | async-start | bytes 4866048 | tf_op jit(solution)/shard_map/all_gather | solution.py:48
  7.9 345.6 %all-gather.5.cloned.1.call-start = ((), (), s32[]{:S(2)}) async-start(), calls=%async_computation.3 | async-start | bytes 4866048 | tf_op jit(solution)/shard_map/all_gather | solution.py:49
  7.9 38.6 %collective-permute-start = (bf16[1,128,6144]{2,1,0:T(8,128)(2,1)}, bf16[1,128,6144]{2,1,0:T(8,128)(2,1)S(1)}, u32[]{:S(2)}, u32[]{:S(2)}) collective-permute-start(bf16[1,128,6144]{2,1,0:T(8,128)(2,1)} %param.7), channel_id=1, source_target_pairs={{0,32},{32,64},{64,96},{96,128},{128,160},{160,192},{192,224},{224... | collective-permute-start | bytes 4718600 | tf_op jit(solution)/shard_map/ppermute | solution.py:14
  13.2 189.9 %copy-start.3 = (u32[256]{0:T(256)S(1)}, u32[256]{0:T(256)}, u32[]{:S(2)}) copy-start(u32[256]{0:T(256)} %constant.77) | copy-start | bytes 3076
  13.2 191.2 %copy-start.4 = (bf16[1,192]{1,0:T(2,128)(2,1)S(1)}, bf16[1,192]{1,0:T(2,128)(2,1)}, u32[]{:S(2)}) copy-start(bf16[1,192]{1,0:T(2,128)(2,1)} %param.12) | copy-start | bytes 1156
  46.9 81.7 %collective-permute-start.1 = (bf16[2,128,6144]{2,1,0:T(8,128)(2,1)S(1)}, bf16[2,128,6144]{2,1,0:T(8,128)(2,1)}, u32[]{:S(2)}, u32[]{:S(2)}) collective-permute-start(bf16[2,128,6144]{2,1,0:T(8,128)(2,1)S(1)} %pad_maximum_fusion), channel_id=1, source_target_pairs={{0,32},{32,0},{64,96},{96,64},{128,160},{160,128},{192,224},{224,1... | collective-permute-start | bytes 9437192 | tf_op jit(solution)/shard_map/ppermute | solution.py:24
  128.6 68.3 %collective-permute-start.2 = (bf16[2,128,6144]{2,1,0:T(8,128)(2,1)}, bf16[2,128,6144]{2,1,0:T(8,128)(2,1)}, u32[]{:S(2)}, u32[]{:S(2)}) collective-permute-start(bf16[2,128,6144]{2,1,0:T(8,128)(2,1)} %collective-permute-done.1), channel_id=1, source_target_pairs={{0,64},{64,0},{32,96},{96,32},{128,192},{192,128},{160,224},{224,1... | collective-permute-start | bytes 9437192 | tf_op jit(solution)/shard_map/ppermute | solution.py:24
  129.5 386.5 %reduce-scatter.3.cloned.1.call-start = ((), (), s32[]{:S(2)}) async-start(), calls=%async_computation.4 | async-start | bytes 4866048 | tf_op jit(solution)/shard_map/reduce_scatter | solution.py:110
  196.9 142.2 %collective-permute-start.3 = (bf16[2,128,6144]{2,1,0:T(8,128)(2,1)}, bf16[2,128,6144]{2,1,0:T(8,128)(2,1)}, u32[]{:S(2)}, u32[]{:S(2)}) collective-permute-start(bf16[2,128,6144]{2,1,0:T(8,128)(2,1)} %collective-permute-done.2), channel_id=1, source_target_pairs={{0,128},{128,0},{32,160},{160,32},{64,192},{192,64},{96,224},{224,... | collective-permute-start | bytes 9437192 | tf_op jit(solution)/shard_map/ppermute | solution.py:24
  199.8 153.7 %collective-permute-start.4 = (bf16[1,128,6144]{2,1,0:T(8,128)(2,1)}, bf16[1,128,6144]{2,1,0:T(8,128)(2,1)S(1)}, u32[]{:S(2)}, u32[]{:S(2)}) collective-permute-start(bf16[1,128,6144]{2,1,0:T(8,128)(2,1)} %param.8), channel_id=1, source_target_pairs={{0,224},{32,0},{64,32},{96,64},{128,96},{160,128},{192,160},{224,1... | collective-permute-start | bytes 4718600 | tf_op jit(solution)/shard_map/ppermute | solution.py:14
  353.5 3.5 copy-start.2
  360.7 274.5 %reduce-scatter.5.cloned.1.call-start = ((), (), s32[]{:S(2)}) async-start(), calls=%async_computation.5 | async-start | bytes 4866048 | tf_op jit(solution)/shard_map/reduce_scatter | solution.py:113
  503.4 5.3 copy-start
  503.4 9.2 %slice-start = ((s8[6291456]{0:T(1024)(128)(4,1)}), s8[4194304]{0:T(1024)(128)(4,1)S(1)}, s32[]{:S(2)}) async-start(s8[6291456]{0:T(1024)(128)(4,1)} %bitcast.70), calls=%async_computation.6 | async-start | bytes 8388608
  508.8 3.9 slice-start.1
  510.7 3.1 copy-start.1
Sparse Core Ops, SparseCore 0:
  10.8 117.8 all-gather.2
  131.4 85.5 all-gather.4
  360.8 141.1 reduce-scatter.2
  506.7 128.4 reduce-scatter.4
where the time goes:
time: 648 us; the launch traced here: 643 us
  waiting for transfers between devices  300 us (46%)
  blocking collectives  262 us (40%)
  matrix products  29.5 us (5%)
  between operations  19.7 us (3%)
  other arithmetic  18.9 us (3%)
  starting transfers between devices  8.76 us (1%)
    unnamed x2, blocking collectives  262 us
    ppermute x3, waiting for transfers between devices, partner_2(): return lax.ppermute(block, axis, route)  148 us
    reduce_scatter x1, waiting for transfers between devices, per_device(): lax.psum_scatter(part_out.astype(jnp.bfloat16), 'dp', scatter_dimension=1...  118 us
    ppermute x2, waiting for transfers between devices, from_behind(): return lax.ppermute(value, axis, pairs)  33.4 us
  transfers between devices with their start and end apart: 9, of which 4 were waited for; matrix products, arithmetic and copies ran while one was open for 7% of the time, Pallas kernels for 0%

commit v1 on v0

v1 whole, which is shorter than its diff:
```python
import jax
import jax.numpy as jnp
from jax import lax
from jax.experimental import pallas as pl
from jax.experimental.pallas import tpu as pltpu
from jax.sharding import PartitionSpec as P

EPSILON = 1e-05
MESH = pl.DeviceIdType.MESH
F32 = jnp.float32
BF16 = jnp.bfloat16
ROWS_IN_COMMON = (((0,), (0,)), ((), ()))
COLS_IN_COMMON = (((1,), (1,)), ((), ()))

NZ = 8
HALF = 192
CHIP = 2 * HALF
PACK = 2 * HALF + 16

CHAINS = ((1, 0, 4), (-1, 1, 4), (1, 1, 3), (-1, 0, 3))
FIRST = (0, 4, 8, 11)
STEPS = 14


def remote(src, dst, send_sem, recv_sem, section, dp):
    return pltpu.make_async_remote_copy(
        src_ref=src,
        dst_ref=dst,
        send_sem=send_sem,
        recv_sem=recv_sem,
        device_id=(section, dp),
        device_id_type=MESH,
    )


def gelu_and_slope(x):
    c = 0.7978845608028654
    a = 0.044715
    t = jnp.tanh(c * (x + a * (x * x * x)))
    hidden = x * (0.5 * (1.0 + t))
    slope = 0.5 * (1.0 + t) + 0.5 * x * (1.0 - t * t) * (c * (1.0 + 3.0 * a * (x * x)))
    return hidden, slope


def tick_kernel(
    shard,
    plan,
    act,
    grad,
    pool,
    act_next,
    grad_next,
    pool_next,
    sums,
    w,
    part,
    sib_part,
    chain_in,
    last_in,
    slots,
    wanted,
    stash,
    up,
    xin,
    pin,
    normed,
    d_unit,
    out_act,
    ring_send,
    ring_recv,
    sib_send,
    sib_recv,
    y_send,
    y_recv,
    sec_send,
    sec_recv,
    chain_send,
    chain_recv,
    half_send,
    half_recv,
    last_send,
    last_recv,
    local,
):
    rows, width = act.shape
    chips = width // CHIP
    s = lax.axis_index("section")
    d = lax.axis_index("dp")
    core = d % 2
    y = (d // 2) % 2
    z = d // 4
    sections = lax.axis_size("section")
    after = (s + 1) % sections
    before = (s + sections - 1) % sections
    partner = sections - 1 - s
    across = (2 * sections - 2 - s) % sections
    sibling = z * 4 + y * 2 + (1 - core)
    other_y = z * 4 + (1 - y) * 2 + core

    def z_of(step):
        return (z + step + 2 * NZ) % NZ

    def dp_of(step):
        return z_of(step) * 4 + y * 2 + core

    def flipped(bit):
        return (y + bit) % 2

    load_slots = pltpu.make_async_copy(pool, slots, local.at[0])
    load_slots.start()
    keep_shard = pltpu.make_async_copy(shard, w.at[d], local.at[1])
    keep_shard.start()

    barrier = pltpu.get_barrier_semaphore()
    for target in (
        (s, sibling),
        (s, other_y),
        (s, dp_of(1)),
        (s, dp_of(-1)),
        (after, d),
        (before, d),
        (partner, d),
    ):
        pl.semaphore_signal(barrier, inc=1, device_id=target, device_id_type=MESH)

    @pl.when(across != s)
    def _():
        pl.semaphore_signal(barrier, inc=1, device_id=(across, d), device_id_type=MESH)
        pl.semaphore_wait(barrier, 8)

    @pl.when(across == s)
    def _():
        pl.semaphore_wait(barrier, 7)

    def gather_copy(i, k, src=None):
        direction, bit, _ = CHAINS[i]
        slot = z_of(-direction * k) * 4 + flipped(bit) * 2 + core
        return remote(
            w.at[slot] if src is None else src,
            w.at[slot],
            ring_send.at[FIRST[i] + k],
            ring_recv.at[FIRST[i] + k],
            s,
            dp_of(direction),
        )

    def gathered(i, k):
        direction, bit, _ = CHAINS[i]
        slot = z_of(-direction * (k + 1)) * 4 + flipped(bit) * 2 + core
        return slot, remote(
            w.at[slot],
            w.at[slot],
            ring_send.at[FIRST[i] + k],
            ring_recv.at[FIRST[i] + k],
            s,
            dp_of(direction),
        )

    def to_sibling(slot, index, src=None):
        return remote(
            w.at[slot] if src is None else src,
            w.at[slot],
            sib_send.at[index],
            sib_recv.at[index],
            s,
            sibling,
        )

    def from_sibling(slot, index):
        other = slot + 1 - 2 * core
        return remote(w.at[other], w.at[other], sib_send.at[index], sib_recv.at[index], s, sibling)

    exchange = remote(shard, w.at[d], y_send.at[0], y_recv.at[0], s, other_y)
    exchange.start()
    sends = [exchange, gather_copy(0, 0, shard), gather_copy(3, 0, shard), to_sibling(d, 14, shard)]
    for copy in sends[1:]:
        copy.start()

    grad_copy = remote(grad, up, sec_send.at[0], sec_recv.at[0], before, d)
    grad_copy.start()

    load_slots.wait()
    mine_fetch = plan[s, 0]
    mine_keep = plan[s, 1]
    theirs_fetch = plan[partner, 0]
    theirs_keep = plan[partner, 1]

    def pick(c, carry):
        at = pl.ds(pl.multiple_of(c * CHIP, 128), CHIP)
        first = slots[0, :, at].astype(F32)
        second = slots[1, :, at].astype(F32)
        wanted[:, at] = jnp.where(theirs_fetch >= 3, second, first).astype(BF16)
        return carry

    lax.fori_loop(0, chips, pick, 0)
    wanted_copy = remote(wanted, stash, sec_send.at[1], sec_recv.at[1], partner, d)
    wanted_copy.start()

    slot_y = z * 4 + (1 - y) * 2 + core
    remote(w.at[slot_y], w.at[slot_y], y_send.at[0], y_recv.at[0], s, other_y).wait_recv()
    more = [gather_copy(1, 0), gather_copy(2, 0), to_sibling(slot_y, 15)]
    for copy in more:
        copy.start()
    sends += more
    sib_slots = [(d, 14), (slot_y, 15)]
    for k in range(4):
        for i, (_, _, hops) in enumerate(CHAINS):
            if k >= hops:
                continue
            slot, arrival = gathered(i, k)
            arrival.wait_recv()
            if k + 1 < hops:
                copy = gather_copy(i, k + 1)
                copy.start()
                sends.append(copy)
            copy = to_sibling(slot, FIRST[i] + k)
            copy.start()
            sends.append(copy)
            sib_slots.append((slot, FIRST[i] + k))
    for slot, index in sib_slots:
        from_sibling(slot, index).wait_recv()
    keep_shard.wait()

    def w_in_of(c):
        return jnp.concatenate([w[2 * c, :HALF, :], w[2 * c + 1, :HALF, :]], axis=0)

    def w_out_of(c):
        return jnp.concatenate([w[2 * c, HALF:CHIP, :], w[2 * c + 1, HALF:CHIP, :]], axis=0)

    def gain_of(c):
        both = w[2 * c, CHIP:PACK, :].astype(F32) + w[2 * c + 1, CHIP:PACK, :].astype(F32)
        return both[:1]

    def lanes(c):
        return pl.ds(pl.multiple_of(c * CHIP, 128), CHIP)

    def folded(v):
        return v[:, :128] + v[:, 128:256] + v[:, 256:]

    def stats(ref):
        zero = jnp.zeros((rows, 128), F32)
        total = lax.fori_loop(
            0, chips, lambda c, acc: acc + folded(ref[:, lanes(c)].astype(F32)), zero
        )
        mean = jnp.sum(total, axis=1, keepdims=True) / width

        def spread(c, acc):
            centred = ref[:, lanes(c)].astype(F32) - mean
            return acc + folded(centred * centred)

        total = lax.fori_loop(0, chips, spread, zero)
        inverse = lax.rsqrt(jnp.sum(total, axis=1, keepdims=True) / width + EPSILON)
        return mean, inverse

    wanted_copy.wait_recv()

    def choose(c, carry):
        at = lanes(c)
        own = jnp.where(mine_fetch >= 1, slots[1, :, at].astype(F32), slots[0, :, at].astype(F32))
        stash[:, at] = jnp.where(mine_fetch >= 2, stash[:, at].astype(F32), own).astype(BF16)
        return carry

    lax.fori_loop(0, chips, choose, 0)
    mean_z, inverse_z = stats(stash)
    grad_copy.wait_recv()

    act_copy = remote(act, xin, sec_send.at[2], sec_recv.at[2], after, d)
    act_copy.start()
    pin_copy = remote(act, pin, sec_send.at[3], sec_recv.at[3], across, d)
    pin_local = pltpu.make_async_copy(act, pin, local.at[2])

    @pl.when(across != s)
    def _():
        pin_copy.start()

    @pl.when(across == s)
    def _():
        pin_local.start()

    def pre_step(c, carry):
        pre, d_hidden = carry
        at = lanes(c)
        unit = (stash[:, at].astype(F32) - mean_z) * inverse_z
        rounded = (unit * gain_of(c)).astype(BF16)
        normed[:, at] = rounded
        pre += jnp.dot(rounded, w_in_of(c), preferred_element_type=F32)
        d_hidden += jnp.dot(up[:, at], w_out_of(c), preferred_element_type=F32)
        return pre, d_hidden

    zero = jnp.zeros((rows, CHIP), F32)
    pre, d_hidden = lax.fori_loop(0, chips, pre_step, (zero, zero))
    hidden, slope = gelu_and_slope(pre)
    hidden = hidden.astype(BF16)
    d_pre = (d_hidden * slope).astype(BF16)

    def half_copy(chip):
        return remote(
            part.at[chip, 1 - core],
            sib_part.at[chip],
            half_send.at[chip],
            half_recv.at[chip],
            s,
            sibling,
        )

    def chip_at(i, k):
        direction, bit, hops = CHAINS[i]
        return z_of(direction * (hops - k)) * 2 + flipped(bit)

    order = [chip_at(i, k) for k in range(4) for i in range(4) if k < CHAINS[i][2]]
    own_far = z * 2 + flipped(1)
    own_near = z * 2 + y
    order += [own_far, own_near]

    def partials(chip, row_sums):
        at = lanes(chip)
        rounded = normed[:, at]
        u = up[:, at]
        p_in = lax.dot_general(rounded, d_pre, ROWS_IN_COMMON, preferred_element_type=F32)
        p_out = lax.dot_general(u, hidden, ROWS_IN_COMMON, preferred_element_type=F32)
        p_in = p_in.astype(BF16)
        p_out = p_out.astype(BF16)
        d_normed = lax.dot_general(d_pre, w_in_of(chip), COLS_IN_COMMON, preferred_element_type=F32)
        unit = (stash[:, at].astype(F32) - mean_z) * inverse_z
        p_gain = jnp.sum(d_normed * unit, axis=0, keepdims=True)
        p_gain = jnp.broadcast_to(p_gain, (16, CHIP)).astype(BF16)
        for half in range(2):
            part[chip, half, :HALF, :] = p_in[half * HALF : (half + 1) * HALF]
            part[chip, half, HALF:CHIP, :] = p_out[half * HALF : (half + 1) * HALF]
            part[chip, half, CHIP:PACK, :] = p_gain
        half_copy(chip).start()
        d_u = d_normed * gain_of(chip)
        d_unit[:, at] = d_u
        return row_sums[0] + folded(d_u), row_sums[1] + folded(d_u * unit)

    row_sums = (jnp.zeros((rows, 128), F32), jnp.zeros((rows, 128), F32))

    def chain_copy(i, k):
        return remote(
            part.at[chip_at(i, k), core],
            chain_in.at[FIRST[i] + k],
            chain_send.at[FIRST[i] + k],
            chain_recv.at[FIRST[i] + k],
            s,
            dp_of(CHAINS[i][0]),
        )

    def chip_sum(chip, *arrived):
        half_copy(chip).wait_recv()
        total = part[chip, core].astype(F32) + sib_part[chip].astype(F32)
        for index in arrived:
            total += chain_in[index].astype(F32)
        return total

    def chain_step(i, k):
        chip = chip_at(i, k)
        arrived = ()
        if k > 0:
            chain_copy(i, k - 1).wait_recv()
            arrived = (FIRST[i] + k - 1,)
        part[chip, core] = chip_sum(chip, *arrived).astype(BF16)
        chain_copy(i, k).start()

    entries = [(i, k) for k in range(4) for i in range(4) if k < CHAINS[i][2]]
    for chip in order:
        row_sums = partials(chip, row_sums)
    for i, k in entries:
        chain_step(i, k)

    mean_d = jnp.sum(row_sums[0], axis=1, keepdims=True) / width
    mean_du = jnp.sum(row_sums[1], axis=1, keepdims=True) / width

    def input_grad(c, carry):
        at = lanes(c)
        unit = (stash[:, at].astype(F32) - mean_z) * inverse_z
        change = inverse_z * (d_unit[:, at] - mean_d - unit * mean_du)
        normed[:, at] = (up[:, at].astype(F32) + change).astype(BF16)
        return carry

    lax.fori_loop(0, chips, input_grad, 0)
    store_grad = pltpu.make_async_copy(normed, grad_next, local.at[3])
    store_grad.start()

    for i in (1, 2):
        chain_copy(i, CHAINS[i][2] - 1).wait_recv()
    part[own_far, core] = chip_sum(
        own_far, FIRST[1] + CHAINS[1][2] - 1, FIRST[2] + CHAINS[2][2] - 1
    ).astype(BF16)
    last_copy = remote(
        part.at[own_far, core], last_in, last_send.at[0], last_recv.at[0], s, other_y
    )
    last_copy.start()

    act_copy.wait_recv()
    mean_x, inverse_x = stats(xin)

    def pre_x_step(c, pre_x):
        unit = (xin[:, lanes(c)].astype(F32) - mean_x) * inverse_x
        rounded = (unit * gain_of(c)).astype(BF16)
        return pre_x + jnp.dot(rounded, w_in_of(c), preferred_element_type=F32)

    hidden_x, _ = gelu_and_slope(lax.fori_loop(0, chips, pre_x_step, zero))
    hidden_x = hidden_x.astype(BF16)

    def forward_step(c, carry):
        at = lanes(c)
        added = lax.dot_general(hidden_x, w_out_of(c), COLS_IN_COMMON, preferred_element_type=F32)
        out_act[:, at] = (xin[:, at].astype(F32) + added).astype(BF16)
        return carry

    lax.fori_loop(0, chips, forward_step, 0)
    store_act = pltpu.make_async_copy(out_act, act_next, local.at[4])
    store_act.start()

    @pl.when(across != s)
    def _():
        pin_copy.wait()

    @pl.when(across == s)
    def _():
        pin_local.wait()

    def keep(c, carry):
        at = lanes(c)
        for j in range(2):
            value = jnp.where(
                theirs_keep == j + 2, pin[:, at].astype(F32), slots[j, :, at].astype(F32)
            )
            slots[j, :, at] = jnp.where(mine_keep == j, xin[:, at].astype(F32), value).astype(BF16)
        return carry

    lax.fori_loop(0, chips, keep, 0)
    store_pool = pltpu.make_async_copy(slots, pool_next, local.at[5])
    store_pool.start()

    for i in (0, 3):
        chain_copy(i, CHAINS[i][2] - 1).wait_recv()
    total = chip_sum(own_near, FIRST[0] + CHAINS[0][2] - 1, FIRST[3] + CHAINS[3][2] - 1)
    last_copy.wait_recv()
    sums[...] = total + last_in[...].astype(F32)

    for copy in sends:
        copy.wait_send()
    grad_copy.wait_send()
    wanted_copy.wait_send()
    act_copy.wait_send()
    for chip in order:
        half_copy(chip).wait_send()
    for i, k in entries:
        chain_copy(i, k).wait_send()
    last_copy.wait_send()
    store_grad.wait()
    store_act.wait()
    store_pool.wait()


def per_device(act_sent, grad_sent, stash_pool, w_in, w_out, gain, plan):
    rows, width = act_sent.shape[1:]
    core = lax.axis_index("dp") % 2
    gain_row = jnp.tile(gain, (1, 2))
    lane = lax.broadcasted_iota(jnp.int32, gain_row.shape, 1)
    gain_row = jnp.where(lane // HALF == core, gain_row, jnp.zeros_like(gain_row))
    shard = jnp.concatenate(
        [w_in[0], w_out[0].T, jnp.broadcast_to(gain_row, (16, CHIP))], axis=0
    )
    anywhere = pl.BlockSpec(memory_space=pl.ANY)
    vmem = pl.BlockSpec(memory_space=pltpu.VMEM)
    block = jax.ShapeDtypeStruct((rows, width), BF16)
    chips = width // CHIP
    dma = pltpu.SemaphoreType.DMA
    act_next, grad_next, pool_next, sums = pl.pallas_call(
        tick_kernel,
        out_shape=(
            block,
            block,
            jax.ShapeDtypeStruct((2, rows, width), BF16),
            jax.ShapeDtypeStruct((PACK, CHIP), F32),
        ),
        in_specs=[
            vmem,
            pl.BlockSpec(memory_space=pltpu.SMEM),
            anywhere,
            anywhere,
            anywhere,
        ],
        out_specs=(anywhere, anywhere, anywhere, vmem),
        scratch_shapes=[
            pltpu.VMEM((2 * chips, PACK, CHIP), BF16),
            pltpu.VMEM((chips, 2, PACK, CHIP), BF16),
            pltpu.VMEM((chips, PACK, CHIP), BF16),
            pltpu.VMEM((STEPS, PACK, CHIP), BF16),
            pltpu.VMEM((PACK, CHIP), BF16),
            pltpu.VMEM((2, rows, width), BF16),
            pltpu.VMEM((rows, width), BF16),
            pltpu.VMEM((rows, width), BF16),
            pltpu.VMEM((rows, width), BF16),
            pltpu.VMEM((rows, width), BF16),
            pltpu.VMEM((rows, width), BF16),
            pltpu.VMEM((rows, width), BF16),
            pltpu.VMEM((rows, width), F32),
            pltpu.VMEM((rows, width), BF16),
            dma((STEPS,)),
            dma((STEPS,)),
            dma((16,)),
            dma((16,)),
            dma((1,)),
            dma((1,)),
            dma((4,)),
            dma((4,)),
            dma((STEPS,)),
            dma((STEPS,)),
            dma((chips,)),
            dma((chips,)),
            dma((1,)),
            dma((1,)),
            dma((6,)),
        ],
        compiler_params=pltpu.CompilerParams(
            collective_id=0, has_side_effects=True, vmem_limit_bytes=60 * 1024 * 1024
        ),
        cost_estimate=pl.CostEstimate(
            flops=14 * rows * width * CHIP, bytes_accessed=20 * rows * width, transcendentals=0
        ),
    )(shard, plan, act_sent[0], grad_sent[0], stash_pool[0])
    sum_gain = lax.dynamic_slice_in_dim(sums[CHIP], core * HALF, HALF)
    return (
        act_next[None],
        grad_next[None],
        pool_next[None],
        sums[None, :HALF],
        sums[HALF:CHIP].T[None],
        sum_gain[None],
    )


def solution(mesh):
    placed = (
        P("section", "dp", None),
        P("section", "dp", None),
        P("section", None, "dp", None),
        P("section", "dp", None),
        P("section", None, "dp"),
        P("section", "dp"),
        P(),
    )
    return jax.shard_map(
        per_device,
        mesh=mesh,
        in_specs=placed,
        out_specs=(
            P("section", "dp", None),
            P("section", "dp", None),
            P("section", None, "dp", None),
            P("section", "dp", None),
            P("section", None, "dp"),
            P("section", "dp"),
        ),
        check_vma=False,
    )
```

time: 648 us -> 221 us (0.34)
  waiting for transfers between devices: 300 us -> 0 us
  blocking collectives: 262 us -> 0 us
  Pallas kernels: 0 us -> 202 us
  matrix products: 29.5 us -> 0 us
  between operations: 19.7 us -> 0.67 us
  other arithmetic: 18.9 us -> 2.44 us
  starting transfers between devices: 8.76 us -> 0 us
  local copies, waits for them, and re-layouts: 4.87 us -> 11.6 us
    unnamed x2 -> x0, blocking collectives: 262 us -> none
    pallas_call x0 -> x1, Pallas kernels: none -> 202 us  [per_device(): pl.pallas_call(tick_kernel, out_shape=(block, block, jax.ShapeDtypeStruct...]
    ppermute x5 -> x0, waiting for transfers between devices: 181 us -> none  [the longest x3 148 us: partner_2(): return lax.ppermute(block, axis, route)]
    reduce_scatter x2 -> x0, waiting for transfers between devices: 118 us -> none  [the longest x1 118 us: per_device(): lax.psum_scatter(part_out.astype(jnp.bfloat16), 'dp', scatter_dimension=1...]
    dot_general x6 -> x0, matrix products: 29.5 us -> none  [the longest x1 6.72 us: per_device(): lax.dot_general(d_pre, w_in_full, CONTRACT_COLS, preferred_element_type=j...]
    ppermute x5 -> x0, starting transfers between devices: 8.43 us -> none  [the longest x3 4.74 us: partner_2(): return lax.ppermute(block, axis, route)]
    broadcast_in_dim x5 -> x0, other arithmetic: 8.14 us -> none  [the longest x1 2.27 us: per_device(): backward[None]]
  transfers between devices with their start and end apart: 9 -> 0, of which waited for: 4 -> 0; matrix products, arithmetic and copies ran while one was open for 7% -> 0% of each run, Pallas kernels for 0% -> 0%
where the time goes in v1:
time: 221 us; the launch traced here: 217 us
  Pallas kernels  202 us (91%)
  local copies, waits for them, and re-layouts  11.6 us (5%)
  other arithmetic  2.44 us (1%)
    pallas_call x1, Pallas kernels, per_device(): pl.pallas_call(tick_kernel, out_shape=(block, block, jax.ShapeDtypeStruct...  202 us
    unnamed x8, local copies, waits for them, and re-layouts  8.28 us

profile of v1, /device:TPU:224, one launch (start us, length us, event | category | flops | bytes accessed | tf_op | source)
XLA Modules:
  0.0 216.9 jit_solution(1844487921353648040)
XLA Ops:
  0.6 0.7 reduce
  1.4 0.1 tile.13
  1.5 1.3 copy.13.plan
  2.8 1.7 pad_maximum_fusion.shard
  4.5 202.1 %shard_map.118 = (bf16[128,6144]{1,0:T(8,128)(2,1)}, bf16[128,6144]{1,0:T(8,128)(2,1)}, bf16[2,128,6144]{2,1,0:T(8,128)(2,1)}, f32[400,384]{1,0:T(8,128)}) custom-call(bf16[400,384]{1,0:T(8,128)(2,1)} %pad_maximum_fusion.shard, s32[8,2]{1,0:T(8,128)} %copy.13.plan, bf16[128,6144]{1,0:T(8,128)(2,1)} %bitcast.22, bf16[128,6144]{1,0:T(8,128)(2,1)} %bitcast.23, ...), custom_call_target="tpu_custom_call" | custom-call | flops 4227858432 | bytes 15728640 | tf_op jit(solution)/shard_map/pallas_call | solution.py:471
  206.7 0.7 slice.11
  207.4 1.9 slice_bitcast_fusion
  209.3 0.6 constant_dynamic-slice_fusion
  209.9 0.0 copy-start.1
  209.9 2.8 %copy.17 = bf16[1,128,6144]{2,1,0:T(8,128)(2,1)} copy(bf16[1,128,6144]{2,1,0:T(8,128)(2,1)} %bitcast.18) | data formatting | bytes 3145728
  212.7 0.0 copy-done.1
  212.7 0.0 copy-start
  212.7 1.1 copy.18
  213.9 1.3 copy-done
  215.2 1.7 copy.19
  (3 shorter events, 0.0 us)
Async XLA Ops:
  209.9 2.8 %copy-start.1 = (bf16[128,6144]{1,0:T(8,128)(2,1)S(1)}, bf16[128,6144]{1,0:T(8,128)(2,1)}, u32[]{:S(2)}) copy-start(bf16[128,6144]{1,0:T(8,128)(2,1)} %get-tuple-element.11) | copy-start | bytes 4718596
  212.7 2.5 %copy-start = (bf16[2,128,6144]{2,1,0:T(8,128)(2,1)S(1)}, bf16[2,128,6144]{2,1,0:T(8,128)(2,1)}, u32[]{:S(2)}) copy-start(bf16[2,128,6144]{2,1,0:T(8,128)(2,1)} %get-tuple-element.12) | copy-start | bytes 9437188

commit v2 on v1

--- a/solution.py
+++ b/solution.py
@@ -20,6 +20,8 @@
 CHAINS = ((1, 0, 4), (-1, 1, 4), (1, 1, 3), (-1, 0, 3))
 FIRST = (0, 4, 8, 11)
 STEPS = 14
+SLICES = 8
+PIECES = 4
 
 
 def remote(src, dst, send_sem, recv_sem, section, dp):
@@ -72,8 +74,14 @@
     sib_recv,
     y_send,
     y_recv,
-    sec_send,
-    sec_recv,
+    grad_send,
+    grad_recv,
+    wanted_send,
+    wanted_recv,
+    act_send,
+    act_recv,
+    pin_send,
+    pin_recv,
     chain_send,
     chain_recv,
     half_send,
@@ -176,9 +184,6 @@
     for copy in sends[1:]:
         copy.start()
 
-    grad_copy = remote(grad, up, sec_send.at[0], sec_recv.at[0], before, d)
-    grad_copy.start()
-
     load_slots.wait()
     mine_fetch = plan[s, 0]
     mine_keep = plan[s, 1]
@@ -193,17 +198,22 @@
         return carry
 
     lax.fori_loop(0, chips, pick, 0)
-    wanted_copy = remote(wanted, stash, sec_send.at[1], sec_recv.at[1], partner, d)
-    wanted_copy.start()
+
+    def wanted_copy(n):
+        at = pl.ds(n * (rows // PIECES), rows // PIECES)
+        return remote(wanted.at[at], stash.at[at], wanted_send.at[n], wanted_recv.at[n], partner, d)
+
 
     slot_y = z * 4 + (1 - y) * 2 + core
     remote(w.at[slot_y], w.at[slot_y], y_send.at[0], y_recv.at[0], s, other_y).wait_recv()
+    for n in range(PIECES):
+        wanted_copy(n).start()
     more = [gather_copy(1, 0), gather_copy(2, 0), to_sibling(slot_y, 15)]
     for copy in more:
         copy.start()
     sends += more
     sib_slots = [(d, 14), (slot_y, 15)]
-    for k in range(4):
+    def gather_round(k):
         for i, (_, _, hops) in enumerate(CHAINS):
             if k >= hops:
                 continue
@@ -217,9 +227,35 @@
             copy.start()
             sends.append(copy)
             sib_slots.append((slot, FIRST[i] + k))
-    for slot, index in sib_slots:
-        from_sibling(slot, index).wait_recv()
-    keep_shard.wait()
+
+    piece = width // PIECES
+
+    def grad_copy(n):
+        at = pl.ds(n * piece, piece)
+        return remote(grad.at[:, at], up.at[:, at], grad_send.at[n], grad_recv.at[n], before, d)
+
+    def act_copy(n):
+        at = pl.ds(n * (rows // SLICES), rows // SLICES)
+        return remote(act.at[at], xin.at[at], act_send.at[n], act_recv.at[n], after, d)
+
+    def pin_copy(n):
+        at = pl.ds(n * (rows // SLICES), rows // SLICES)
+        return remote(act.at[at], pin.at[at], pin_send.at[n], pin_recv.at[n], across, d)
+
+    pin_local = pltpu.make_async_copy(act, pin, local.at[2])
+
+    gather_round(0)
+    gather_round(1)
+    for n in range(PIECES - 1):
+        wanted_copy(n).wait_recv()
+    for n in range(PIECES):
+        grad_copy(n).start()
+
+    @pl.when(across == s)
+    def _():
+        pin_local.start()
+
+    gather_round(2)
 
     def w_in_of(c):
         return jnp.concatenate([w[2 * c, :HALF, :], w[2 * c + 1, :HALF, :]], axis=0)
@@ -252,7 +288,7 @@
         inverse = lax.rsqrt(jnp.sum(total, axis=1, keepdims=True) / width + EPSILON)
         return mean, inverse
 
-    wanted_copy.wait_recv()
+    wanted_copy(PIECES - 1).wait_recv()
 
     def choose(c, carry):
         at = lanes(c)
@@ -262,35 +298,29 @@
 
     lax.fori_loop(0, chips, choose, 0)
     mean_z, inverse_z = stats(stash)
-    grad_copy.wait_recv()
-
-    act_copy = remote(act, xin, sec_send.at[2], sec_recv.at[2], after, d)
-    act_copy.start()
-    pin_copy = remote(act, pin, sec_send.at[3], sec_recv.at[3], across, d)
-    pin_local = pltpu.make_async_copy(act, pin, local.at[2])
-
-    @pl.when(across != s)
-    def _():
-        pin_copy.start()
-
-    @pl.when(across == s)
-    def _():
-        pin_local.start()
-
-    def pre_step(c, carry):
-        pre, d_hidden = carry
+    gather_round(3)
+    for slot, index in sib_slots:
+        from_sibling(slot, index).wait_recv()
+    keep_shard.wait()
+
+    def pre_step(c, pre):
         at = lanes(c)
         unit = (stash[:, at].astype(F32) - mean_z) * inverse_z
         rounded = (unit * gain_of(c)).astype(BF16)
         normed[:, at] = rounded
-        pre += jnp.dot(rounded, w_in_of(c), preferred_element_type=F32)
-        d_hidden += jnp.dot(up[:, at], w_out_of(c), preferred_element_type=F32)
-        return pre, d_hidden
+        return pre + jnp.dot(rounded, w_in_of(c), preferred_element_type=F32)
+
+    def d_hidden_step(c, d_hidden):
+        return d_hidden + jnp.dot(up[:, lanes(c)], w_out_of(c), preferred_element_type=F32)
 
     zero = jnp.zeros((rows, CHIP), F32)
-    pre, d_hidden = lax.fori_loop(0, chips, pre_step, (zero, zero))
-    hidden, slope = gelu_and_slope(pre)
+    hidden, slope = gelu_and_slope(lax.fori_loop(0, chips, pre_step, zero))
     hidden = hidden.astype(BF16)
+    d_hidden = zero
+    for n in range(PIECES):
+        grad_copy(n).wait_recv()
+        first = n * (chips // PIECES)
+        d_hidden = lax.fori_loop(first, first + chips // PIECES, d_hidden_step, d_hidden)
     d_pre = (d_hidden * slope).astype(BF16)
 
     def half_copy(chip):
@@ -307,7 +337,8 @@
         direction, bit, hops = CHAINS[i]
         return z_of(direction * (hops - k)) * 2 + flipped(bit)
 
-    order = [chip_at(i, k) for k in range(4) for i in range(4) if k < CHAINS[i][2]]
+    entries = [(i, k) for k in range(4) for i in (1, 2, 0, 3) if k < CHAINS[i][2]]
+    order = [chip_at(i, k) for i, k in entries]
     own_far = z * 2 + flipped(1)
     own_near = z * 2 + y
     order += [own_far, own_near]
@@ -360,11 +391,20 @@
             arrived = (FIRST[i] + k - 1,)
         part[chip, core] = chip_sum(chip, *arrived).astype(BF16)
         chain_copy(i, k).start()
-
-    entries = [(i, k) for k in range(4) for i in range(4) if k < CHAINS[i][2]]
-    for chip in order:
+        n = entries.index((i, k))
+        if 2 <= n < 2 + SLICES:
+            act_copy(n - 2).start()
+        if 4 <= n < 4 + SLICES:
+
+            @pl.when(across != s)
+            def _():
+                pin_copy(n - 4).start()
+
+    for n, chip in enumerate(order):
         row_sums = partials(chip, row_sums)
-    for i, k in entries:
+        if 1 <= n <= 4:
+            chain_step(*entries[n - 1])
+    for i, k in entries[4:8]:
         chain_step(i, k)
 
     mean_d = jnp.sum(row_sums[0], axis=1, keepdims=True) / width
@@ -380,6 +420,8 @@
     lax.fori_loop(0, chips, input_grad, 0)
     store_grad = pltpu.make_async_copy(normed, grad_next, local.at[3])
     store_grad.start()
+    for i, k in entries[8:]:
+        chain_step(i, k)
 
     for i in (1, 2):
         chain_copy(i, CHAINS[i][2] - 1).wait_recv()
@@ -391,7 +433,8 @@
     )
     last_copy.start()
 
-    act_copy.wait_recv()
+    for n in range(SLICES):
+        act_copy(n).wait_recv()
     mean_x, inverse_x = stats(xin)
 
     def pre_x_step(c, pre_x):
@@ -414,7 +457,8 @@
 
     @pl.when(across != s)
     def _():
-        pin_copy.wait()
+        for n in range(SLICES):
+            pin_copy(n).wait()
 
     @pl.when(across == s)
     def _():
@@ -441,9 +485,11 @@
 
     for copy in sends:
         copy.wait_send()
-    grad_copy.wait_send()
-    wanted_copy.wait_send()
-    act_copy.wait_send()
+    for n in range(PIECES):
+        grad_copy(n).wait_send()
+        wanted_copy(n).wait_send()
+    for n in range(SLICES):
+        act_copy(n).wait_send()
     for chip in order:
         half_copy(chip).wait_send()
     for i, k in entries:
@@ -505,8 +551,14 @@
             dma((16,)),
             dma((1,)),
             dma((1,)),
-            dma((4,)),
-            dma((4,)),
+            dma((PIECES,)),
+            dma((PIECES,)),
+            dma((PIECES,)),
+            dma((PIECES,)),
+            dma((SLICES,)),
+            dma((SLICES,)),
+            dma((SLICES,)),
+            dma((SLICES,)),
             dma((STEPS,)),
             dma((STEPS,)),
             dma((chips,)),

time: 221 us -> 189 us (0.86); the launches traced: 217 us -> 188 us
  Pallas kernels: 202 us -> 173 us
    pallas_call x1, Pallas kernels: 202 us -> 173 us  [per_device(): pl.pallas_call(tick_kernel, out_shape=(block, block, jax.ShapeDtypeStruct...]
where the time goes in v2:
time: 189 us; the launch traced here: 188 us
  Pallas kernels  173 us (92%)
  local copies, waits for them, and re-layouts  11.6 us (6%)
  other arithmetic  2.44 us (1%)
    pallas_call x1, Pallas kernels, per_device(): pl.pallas_call(tick_kernel, out_shape=(block, block, jax.ShapeDtypeStruct...  173 us
    unnamed x8, local copies, waits for them, and re-layouts  8.28 us

profile of v2, /device:TPU:224, one launch (start us, length us, event | category | flops | bytes accessed | tf_op | source)
XLA Modules:
  0.0 187.5 jit_solution(11613823606840667110)
XLA Ops:
  0.6 0.7 reduce
  1.4 0.1 tile.13
  1.5 1.3 copy.13.plan
  2.8 1.7 pad_maximum_fusion.shard
  4.5 172.8 %shard_map.118 = (bf16[128,6144]{1,0:T(8,128)(2,1)}, bf16[128,6144]{1,0:T(8,128)(2,1)}, bf16[2,128,6144]{2,1,0:T(8,128)(2,1)}, f32[400,384]{1,0:T(8,128)}) custom-call(bf16[400,384]{1,0:T(8,128)(2,1)} %pad_maximum_fusion.shard, s32[8,2]{1,0:T(8,128)} %copy.13.plan, bf16[128,6144]{1,0:T(8,128)(2,1)} %bitcast.22, bf16[128,6144]{1,0:T(8,128)(2,1)} %bitcast.23, ...), custom_call_target="tpu_custom_call" | custom-call | flops 4227858432 | bytes 15728640 | tf_op jit(solution)/shard_map/pallas_call | solution.py:517
  177.3 0.7 slice.11
  178.1 1.9 %slice_bitcast_fusion = (f32[1,384,192]{1,2,0:T(8,128)}, f32[1,192,384]{2,1,0:T(8,128)}) fusion(f32[400,384]{1,0:T(8,128)} %get-tuple-element.13), kind=kLoop, calls=%fused_computation.1 | loop fusion | bytes 1179648 | tf_op jit(solution)/shard_map/broadcast_in_dim | solution.py:583
  180.0 0.6 constant_dynamic-slice_fusion
  180.6 0.0 copy-start.1
  180.6 2.8 %copy.17 = bf16[1,128,6144]{2,1,0:T(8,128)(2,1)} copy(bf16[1,128,6144]{2,1,0:T(8,128)(2,1)} %bitcast.18) | data formatting | bytes 3145728
  183.4 0.0 copy-done.1
  183.4 0.0 copy-start
  183.4 1.1 copy.18
  184.6 1.3 copy-done
  185.9 1.7 copy.19
  (3 shorter events, 0.0 us)
Async XLA Ops:
  180.6 2.8 %copy-start.1 = (bf16[128,6144]{1,0:T(8,128)(2,1)S(1)}, bf16[128,6144]{1,0:T(8,128)(2,1)}, u32[]{:S(2)}) copy-start(bf16[128,6144]{1,0:T(8,128)(2,1)} %get-tuple-element.11) | copy-start | bytes 4718596
  183.4 2.5 %copy-start = (bf16[2,128,6144]{2,1,0:T(8,128)(2,1)S(1)}, bf16[2,128,6144]{2,1,0:T(8,128)(2,1)}, u32[]{:S(2)}) copy-start(bf16[2,128,6144]{2,1,0:T(8,128)(2,1)} %get-tuple-element.12) | copy-start | bytes 9437188

commit v3 on v2

--- a/solution.py
+++ b/solution.py
@@ -20,6 +20,7 @@
 CHAINS = ((1, 0, 4), (-1, 1, 4), (1, 1, 3), (-1, 0, 3))
 FIRST = (0, 4, 8, 11)
 STEPS = 14
+ACT_STEPS = (4, 5, 6, 7)
 SLICES = 8
 PIECES = 4
 
@@ -392,15 +393,17 @@
         part[chip, core] = chip_sum(chip, *arrived).astype(BF16)
         chain_copy(i, k).start()
         n = entries.index((i, k))
-        if 2 <= n < 2 + SLICES:
-            act_copy(n - 2).start()
-        if 4 <= n < 4 + SLICES:
+        if n in ACT_STEPS:
+            act_copy(SLICES - len(ACT_STEPS) + ACT_STEPS.index(n)).start()
+        if 6 <= n < 6 + SLICES:
 
             @pl.when(across != s)
             def _():
-                pin_copy(n - 4).start()
+                pin_copy(n - 6).start()
 
     for n, chip in enumerate(order):
+        if n % 4 == 0:
+            act_copy(n // 4).start()
         row_sums = partials(chip, row_sums)
         if 1 <= n <= 4:
             chain_step(*entries[n - 1])

time: 189 us -> 184 us (0.974)
  Pallas kernels: 173 us -> 169 us
    pallas_call x1, Pallas kernels: 173 us -> 169 us  [per_device(): pl.pallas_call(tick_kernel, out_shape=(block, block, jax.ShapeDtypeStruct...]
where the time goes in v3:
time: 184 us; the launch traced here: 183 us
  Pallas kernels  169 us (92%)
  local copies, waits for them, and re-layouts  11.6 us (6%)
  other arithmetic  2.44 us (1%)
    pallas_call x1, Pallas kernels, per_device(): pl.pallas_call(tick_kernel, out_shape=(block, block, jax.ShapeDtypeStruct...  169 us
    unnamed x8, local copies, waits for them, and re-layouts  8.28 us

profile of v3, /device:TPU:224, one launch (start us, length us, event | category | flops | bytes accessed | tf_op | source)
XLA Modules:
  0.0 183.4 jit_solution(7616493073604013037)
XLA Ops:
  0.6 0.7 reduce
  1.4 0.1 tile.13
  1.5 1.3 copy.13.plan
  2.8 1.7 pad_maximum_fusion.shard
  4.5 168.6 %shard_map.118 = (bf16[128,6144]{1,0:T(8,128)(2,1)}, bf16[128,6144]{1,0:T(8,128)(2,1)}, bf16[2,128,6144]{2,1,0:T(8,128)(2,1)}, f32[400,384]{1,0:T(8,128)}) custom-call(bf16[400,384]{1,0:T(8,128)(2,1)} %pad_maximum_fusion.shard, s32[8,2]{1,0:T(8,128)} %copy.13.plan, bf16[128,6144]{1,0:T(8,128)(2,1)} %bitcast.22, bf16[128,6144]{1,0:T(8,128)(2,1)} %bitcast.23, ...), custom_call_target="tpu_custom_call" | custom-call | flops 4227858432 | bytes 15728640 | tf_op jit(solution)/shard_map/pallas_call | solution.py:520
  173.2 0.7 slice.11
  173.9 1.9 %slice_bitcast_fusion = (f32[1,384,192]{1,2,0:T(8,128)}, f32[1,192,384]{2,1,0:T(8,128)}) fusion(f32[400,384]{1,0:T(8,128)} %get-tuple-element.13), kind=kLoop, calls=%fused_computation.1 | loop fusion | bytes 1179648 | tf_op jit(solution)/shard_map/broadcast_in_dim | solution.py:586
  175.8 0.6 constant_dynamic-slice_fusion
  176.4 0.0 copy-start.1
  176.4 2.8 %copy.17 = bf16[1,128,6144]{2,1,0:T(8,128)(2,1)} copy(bf16[1,128,6144]{2,1,0:T(8,128)(2,1)} %bitcast.18) | data formatting | bytes 3145728
  179.2 0.0 copy-done.1
  179.2 0.0 copy-start
  179.3 1.1 copy.18
  180.4 1.3 copy-done
  181.7 1.7 copy.19
  (3 shorter events, 0.0 us)
Async XLA Ops:
  176.4 2.8 %copy-start.1 = (bf16[128,6144]{1,0:T(8,128)(2,1)S(1)}, bf16[128,6144]{1,0:T(8,128)(2,1)}, u32[]{:S(2)}) copy-start(bf16[128,6144]{1,0:T(8,128)(2,1)} %get-tuple-element.11) | copy-start | bytes 4718596
  179.2 2.5 %copy-start = (bf16[2,128,6144]{2,1,0:T(8,128)(2,1)S(1)}, bf16[2,128,6144]{2,1,0:T(8,128)(2,1)}, u32[]{:S(2)}) copy-start(bf16[2,128,6144]{2,1,0:T(8,128)(2,1)} %get-tuple-element.12) | copy-start | bytes 9437188

commit v4 on v3

--- a/solution.py
+++ b/solution.py
@@ -20,7 +20,7 @@
 CHAINS = ((1, 0, 4), (-1, 1, 4), (1, 1, 3), (-1, 0, 3))
 FIRST = (0, 4, 8, 11)
 STEPS = 14
-ACT_STEPS = (4, 5, 6, 7)
+ACT_STEPS = (4, 6)
 SLICES = 8
 PIECES = 4
 
@@ -320,6 +320,8 @@
     d_hidden = zero
     for n in range(PIECES):
         grad_copy(n).wait_recv()
+        if n >= 2:
+            act_copy(n - 2).start()
         first = n * (chips // PIECES)
         d_hidden = lax.fori_loop(first, first + chips // PIECES, d_hidden_step, d_hidden)
     d_pre = (d_hidden * slope).astype(BF16)
@@ -402,8 +404,8 @@
                 pin_copy(n - 6).start()
 
     for n, chip in enumerate(order):
-        if n % 4 == 0:
-            act_copy(n // 4).start()
+        if n in (3, 7, 11, 15):
+            act_copy(2 + n // 4).start()
         row_sums = partials(chip, row_sums)
         if 1 <= n <= 4:
             chain_step(*entries[n - 1])

time: 184 us -> 199 us (1.082)
  Pallas kernels: 169 us -> 182 us
    pallas_call x1, Pallas kernels: 169 us -> 182 us  [per_device(): pl.pallas_call(tick_kernel, out_shape=(block, block, jax.ShapeDtypeStruct...]
where the time goes in v4:
time: 199 us; the launch traced here: 197 us
  Pallas kernels  182 us (91%)
  local copies, waits for them, and re-layouts  11.6 us (6%)
  other arithmetic  2.44 us (1%)
    pallas_call x1, Pallas kernels, per_device(): pl.pallas_call(tick_kernel, out_shape=(block, block, jax.ShapeDtypeStruct...  182 us
    unnamed x8, local copies, waits for them, and re-layouts  8.28 us

profile of v4, /device:TPU:224, one launch (start us, length us, event | category | flops | bytes accessed | tf_op | source)
XLA Modules:
  0.0 197.1 jit_solution(11930605661852991686)
XLA Ops:
  0.6 0.7 reduce
  1.4 0.1 tile.13
  1.5 1.3 copy.13.plan
  2.8 1.7 pad_maximum_fusion.shard
  4.5 182.3 %shard_map.118 = (bf16[128,6144]{1,0:T(8,128)(2,1)}, bf16[128,6144]{1,0:T(8,128)(2,1)}, bf16[2,128,6144]{2,1,0:T(8,128)(2,1)}, f32[400,384]{1,0:T(8,128)}) custom-call(bf16[400,384]{1,0:T(8,128)(2,1)} %pad_maximum_fusion.shard, s32[8,2]{1,0:T(8,128)} %copy.13.plan, bf16[128,6144]{1,0:T(8,128)(2,1)} %bitcast.22, bf16[128,6144]{1,0:T(8,128)(2,1)} %bitcast.23, ...), custom_call_target="tpu_custom_call" | custom-call | flops 4227858432 | bytes 15728640 | tf_op jit(solution)/shard_map/pallas_call | solution.py:522
  186.9 0.7 slice.11
  187.6 1.9 slice_bitcast_fusion
  189.5 0.6 constant_dynamic-slice_fusion
  190.1 0.0 copy-start.1
  190.1 2.8 %copy.17 = bf16[1,128,6144]{2,1,0:T(8,128)(2,1)} copy(bf16[1,128,6144]{2,1,0:T(8,128)(2,1)} %bitcast.18) | data formatting | bytes 3145728
  192.9 0.0 copy-done.1
  192.9 0.0 copy-start
  193.0 1.1 copy.18
  194.1 1.3 copy-done
  195.4 1.7 copy.19
  (3 shorter events, 0.0 us)
Async XLA Ops:
  190.1 2.8 %copy-start.1 = (bf16[128,6144]{1,0:T(8,128)(2,1)S(1)}, bf16[128,6144]{1,0:T(8,128)(2,1)}, u32[]{:S(2)}) copy-start(bf16[128,6144]{1,0:T(8,128)(2,1)} %get-tuple-element.11) | copy-start | bytes 4718596
  192.9 2.5 %copy-start = (bf16[2,128,6144]{2,1,0:T(8,128)(2,1)S(1)}, bf16[2,128,6144]{2,1,0:T(8,128)(2,1)}, u32[]{:S(2)}) copy-start(bf16[2,128,6144]{2,1,0:T(8,128)(2,1)} %get-tuple-element.12) | copy-start | bytes 9437188
